TPU v7x, 128 devices: a whole 4x4x4 slice. The times are simulated.
128 devices in a mesh: dp: 4 (over x), tensor: 2 (over core), expert: 16 (over z, y).
Axes of the slice: x: 4, y: 4, z: 4, core: 2. Of those that a mesh axis runs over, the one named last changes fastest.
Arguments:
- tokens: bfloat16 [8192, 2304], P(('dp', 'tensor', 'expert')), may hold values from -6 to 6
- routes: int32 [8192, 2], P(('dp', 'tensor', 'expert')), may hold values from 0 to 7, all different within a row; in each aligned block of 64 rows (0 to 63, 64 to 127, ...) at most 24 rows name the same one
- gates: float32 [8192, 2], P(('dp', 'tensor', 'expert')), may hold values from 0.2 to 1
- segments: int32 [8192], P(('dp', 'tensor', 'expert')), may hold values from 0 to 31, never falling along the last dimension, each value on 1 to 512 neighbouring positions
- w_gate: bfloat16 [16, 2304, 3840], P('expert', None, ('dp', 'tensor')), may hold values from -0.125 to 0.125
- w_up: bfloat16 [16, 2304, 3840], P('expert', None, ('dp', 'tensor')), may hold values from -0.125 to 0.125
- w_down: bfloat16 [16, 3840, 2304], P('expert', ('dp', 'tensor')), may hold values from -0.0625 to 0.0625
Outputs:
- embedded: bfloat16 [8192, 2304], P(('dp', 'tensor', 'expert'))
- pooled: float32 [32, 2304], replicated
Inputs may be any that keep to these rules, and one draw needn't show every extreme that they name: `routes`: each residue names two different experts. Within the rows of one device no expert is named more than 24 times, and in every draw some expert is named exactly 24 times by the rows of some device. `segments`: sequence numbers never fall along the residues; each sequence has 1 to 512 residues and one has exactly 512.
All inputs are finite; a program needn't handle non-finite values.
Results may differ from a plain program's by a relative error of at most 0.0085.
Values may be sent and summed in bfloat16 or wider, within the bound.
A program may use at most 64 MiB of HBM per device.

v0:
```python
import jax
import jax.numpy as jnp
from jax import lax
from jax.sharding import PartitionSpec as P

EXPERTS = 8
TOP = 2
CAP = 24
epsilon = 1e-06


def norm_tokens(tokens):
    values = tokens.astype(jnp.float32)
    scale = lax.rsqrt(jnp.mean(values * values, axis=1, keepdims=True) + epsilon)
    return (values, (values * scale).astype(jnp.bfloat16))


def slot_numbers(routes):
    flat_routes = routes.reshape(-1)
    onehot = (flat_routes[:, None] == jnp.arange(EXPERTS, dtype=jnp.int32)[None, :]).astype(
        jnp.int32
    )
    before = jnp.cumsum(onehot, axis=0) - onehot
    slot_rank = jnp.sum(before * onehot, axis=1)
    return flat_routes * CAP + slot_rank


def placement_matrix(slot_index, tok_count):
    hits = (jnp.arange(EXPERTS * CAP, dtype=jnp.int32)[:, None] == slot_index[None, :]).astype(
        jnp.int32
    )
    return jnp.sum(hits.reshape(EXPERTS * CAP, tok_count, TOP), axis=2).astype(jnp.bfloat16)


def fan_out(slot_rows, replicas):
    leading = slot_rows.shape[:-2]
    features = slot_rows.shape[-1]
    shaped = slot_rows.reshape(leading + (EXPERTS, CAP, features))
    shaped = jnp.repeat(shaped, replicas, axis=len(leading))
    return shaped.reshape(leading + (EXPERTS * replicas * CAP, features))


def expert_hidden(row_block, w_gate, w_up):
    gate_proj = jnp.einsum("nacd,adf->nacf", row_block, w_gate, preferred_element_type=jnp.float32)
    up_proj = jnp.einsum("nacd,adf->nacf", row_block, w_up, preferred_element_type=jnp.float32)
    return (jax.nn.silu(gate_proj) * up_proj).astype(jnp.bfloat16)


def shards(tokens, routes, gates, segments, w_gate, w_up, w_down):
    tok_count = tokens.shape[0]
    width = tokens.shape[1]
    experts_axis = lax.axis_size("expert")
    per_device = w_gate.shape[0]
    replicas = max(1, experts_axis // EXPERTS)
    plane = lax.axis_size("dp") * lax.axis_size("tensor")
    values, normed = norm_tokens(tokens)
    slot_index = slot_numbers(routes)
    placing = placement_matrix(slot_index, tok_count)
    slot_rows = jnp.dot(placing, normed, preferred_element_type=jnp.float32).astype(jnp.bfloat16)
    send_rows = fan_out(slot_rows, replicas)
    received = lax.all_to_all(send_rows, "expert", split_axis=0, concat_axis=0, tiled=True)
    local_rows = received.reshape(experts_axis, per_device, CAP, width)
    hidden = expert_hidden(
        lax.all_gather(local_rows, ("dp", "tensor"), axis=0, tiled=True), w_gate, w_up
    )
    summed = lax.psum_scatter(
        jnp.einsum("nacf,afd->nacd", hidden, w_down, preferred_element_type=jnp.float32).astype(
            jnp.bfloat16
        ),
        ("dp", "tensor"),
        scatter_dimension=0,
        tiled=True,
    )
    returned = lax.all_to_all(summed, "expert", split_axis=0, concat_axis=0, tiled=True).astype(
        jnp.float32
    )
    expert_out = jnp.sum(returned.reshape(EXPERTS, replicas, CAP, width), axis=1)
    picked = jnp.take(expert_out.reshape(EXPERTS * CAP, width), slot_index, axis=0).reshape(
        tok_count, TOP, width
    )
    mixed = values + jnp.sum(gates[:, :, None] * picked, axis=1)
    embedded = mixed.astype(jnp.bfloat16)
    devices_all = plane * experts_axis
    seq_total = tok_count * devices_all // 256
    seq_hot = (jnp.arange(seq_total, dtype=jnp.int32)[:, None] == segments[None, :]).astype(
        jnp.bfloat16
    )
    seq_sums = jnp.dot(seq_hot, embedded, preferred_element_type=jnp.float32)
    seq_counts = jnp.sum(seq_hot.astype(jnp.float32), axis=1)
    total_sums, total_counts = lax.psum((seq_sums, seq_counts), ("dp", "tensor", "expert"))
    pooled = total_sums / total_counts[:, None]
    return (embedded, pooled)


def solution(mesh):
    placed = (
        P(("dp", "tensor", "expert"), None),
        P(("dp", "tensor", "expert"), None),
        P(("dp", "tensor", "expert"), None),
        P(("dp", "tensor", "expert")),
        P("expert", None, ("dp", "tensor")),
        P("expert", None, ("dp", "tensor")),
        P("expert", ("dp", "tensor"), None),
    )
    return jax.shard_map(
        shards,
        mesh=mesh,
        in_specs=placed,
        out_specs=(P(("dp", "tensor", "expert"), None), P()),
        check_vma=False,
    )
```

profile of v0, /device:TPU:1, one launch (start us, length us, event | category | flops | bytes accessed | tf_op | source)
XLA Modules:
  0.0 430.2 jit_solution(17965702247409334811)
XLA Ops:
  7.2 0.0 copy-start
  7.2 0.0 all-gather.3.cloned.1.call-start
  7.2 0.9 copy.33
  8.1 0.1 reshape.117
  8.3 0.1 fusion.14
  8.4 0.2 reduce_window_sum.11
  8.5 0.2 select_reduce_fusion
  8.7 0.1 reduce_sum.59
  8.9 0.1 copy.34
  8.9 0.7 compare_and_fusion
  9.6 0.1 convert_reduce_fusion.1
  9.7 1.1 fusion.9
  10.9 1.4 convolution_convert_fusion
  12.3 0.1 broadcast_in_dim.13
  12.4 32.4 %all_to_all.14 = bf16[16,24,2304]{2,1,0:T(8,128)(2,1)S(1)} all-to-all(bf16[16,24,2304]{2,1,0:T(8,128)(2,1)S(1)} %bitcast.63), channel_id=1, replica_groups=mesh['dp'=4,'tensor'=2,'expert'=16] {'expert'}, dimensions={0} | all-to-all | bytes 3538944 | tf_op jit(solution)/shard_map/all_to_all | solution.py:61
  44.8 1.5 copy.36
  46.3 0.0 all-gather.3.cloned.1.call-update
  46.3 0.0 reduce-scatter.2.cloned.1.call-start
  46.4 73.1 %all-gather.3.cloned.1.call-done = bf16[128,24,2304]{2,0,1:T(8,128)(2,1)} async-done(((bf16[16,24,2304]{2,0,1:T(8,128)(2,1)}), bf16[128,24,2304]{2,0,1:T(8,128)(2,1)}) %all-gather.3.cloned.1.call-update) | async-done | bytes 14155792 | tf_op jit(solution)/shard_map/all_gather | solution.py:64
  119.5 11.4 %fusion.6 = f32[128,24,480]{0,2,1:T(8,128)S(1)} fusion(bf16[128,24,2304]{2,0,1:T(8,128)(2,1)} %all-gather.3.cloned.1.call-done, bf16[1,2304,480]{1,2,0:T(8,128)(2,1)} %param.12), kind=kOutput, calls=%fused_computation.13 | convolution fusion | flops 6794772480 | bytes 22265856 | tf_op jit(solution)/shard_map/nacd,adf->nacf/dot_general | solution.py:45
  130.9 0.0 copy-done.5
  130.9 0.0 copy-done.6
  130.9 8.1 %fusion = bf16[128,1,24,480]{0,3,2,1:T(8,128)(2,1)S(1)} fusion(f32[128,24,480]{0,2,1:T(8,128)S(1)} %fusion.6, bf16[128,24,2304]{2,0,1:T(8,128)(2,1)S(1)} %copy-done.5, bf16[1,2304,480]{1,2,0:T(8,128)(2,1)S(1)} %copy-done.6), kind=kOutput, calls=%fused_computation.3 | convolution fusion | flops 6803619840 | bytes 25214976 | tf_op jit(solution)/shard_map/nacd,adf->nacf/dot_general | solution.py:44
  139.0 0.0 copy-done
  139.0 10.3 %convert_bitcast_fusion = bf16[128,1,24,2304]{3,0,2,1:T(8,128)(2,1)} fusion(bf16[128,1,24,480]{0,3,2,1:T(8,128)(2,1)S(1)} %fusion, bf16[1,480,2304]{2,1,0:T(8,128)(2,1)S(1)} %copy-done), kind=kOutput, calls=%fused_computation.1 | convolution fusion | flops 6801850368 | bytes 19316736 | tf_op jit(solution)/shard_map/nacf,afd->nacd/dot_general | solution.py:67
  149.2 0.0 reduce-scatter.2.cloned.1.call-update
  149.3 79.5 %reduce-scatter.2.cloned.1.call-done = bf16[16,1,24,2304]{3,0,2,1:T(8,128)(2,1)} async-done(((bf16[128,1,24,2304]{3,0,2,1:T(8,128)(2,1)}), bf16[16,1,24,2304]{3,0,2,1:T(8,128)(2,1)}) %reduce-scatter.2.cloned.1.call-update) | async-done | bytes 1769488 | tf_op jit(solution)/shard_map/reduce_scatter | solution.py:66
  228.8 3.2 copy.37
  232.0 6.9 %all-to-all-start.1 = ((bf16[16,1,24,2304]{3,2,1,0:T(8,128)(2,1)}), bf16[16,1,24,2304]{3,2,1,0:T(8,128)(2,1)}, u32[]{:S(2)}, u32[]{:S(2)}) async-start(bf16[16,1,24,2304]{3,2,1,0:T(8,128)(2,1)} %copy.37), calls=%async_computation.2 | async-start | bytes 3538944 | tf_op jit(solution)/shard_map/all_to_all | solution.py:74
  238.9 0.2 all-reduce.2.cloned.1.call-start
  239.1 0.0 copy-done.2
  239.1 0.1 copy.40
  239.2 0.1 mul.61
  239.3 0.1 copy.35
  239.5 0.1 copy.32
  239.6 23.3 %all-to-all-done.1 = bf16[16,1,24,2304]{3,2,1,0:T(8,128)(2,1)} async-done(((bf16[16,1,24,2304]{3,2,1,0:T(8,128)(2,1)}), bf16[16,1,24,2304]{3,2,1,0:T(8,128)(2,1)}, u32[]{:S(2)}, u32[]{:S(2)}) %all-to-all-start.1) | async-done | bytes 1769504 | tf_op jit(solution)/shard_map/all_to_all | solution.py:74
  262.9 3.2 convert_reduce_fusion
  266.0 4.0 gather_fusion
  270.0 2.0 gather.7
  272.0 3.2 multiply_reduce_fusion
  275.3 1.0 fusion.11
  276.3 0.0 copy-start.1
  276.3 0.9 fusion.17
  277.2 0.0 all-reduce.2.cloned.1.call-update
  277.2 0.1 convert_reduce_fusion.2
  277.4 68.6 %psum.15 = f32[32]{0:T(128)S(1)} all-reduce(f32[32]{0:T(128)S(1)} %convert_reduce_fusion.2), channel_id=1, replica_groups=mesh['dp'=4,'tensor'=2,'expert'=16] {'dp','tensor','expert'}, use_global_device_ids=true, to_apply=%region_9.10 | all-reduce | flops 32 | bytes 256 | tf_op jit(solution)/shard_map/psum | solution.py:90
  346.0 75.9 %all-reduce.2.cloned.1.call-done = f32[32,2304]{1,0:T(8,128)} async-done(((f32[32,2304]{1,0:T(8,128)}), f32[32,2304]{1,0:T(8,128)}) %all-reduce.2.cloned.1.call-update) | async-done | bytes 294928 | tf_op jit(solution)/shard_map/psum | solution.py:90
  421.9 1.8 broadcast_divide_fusion
  (12 shorter events, 0.0 us)
Async XLA Ops:
  7.2 131.8 %copy-start = (bf16[1,480,2304]{2,1,0:T(8,128)(2,1)S(1)}, bf16[1,480,2304]{2,1,0:T(8,128)(2,1)}, u32[]{:S(2)}) copy-start(bf16[1,480,2304]{2,1,0:T(8,128)(2,1)} %param.13) | copy-start | bytes 6635524
  7.2 112.3 %all-gather.3.cloned.1.call-start = ((), (), s32[]{:S(2)}) async-start(), calls=%async_computation.5 | async-start | bytes 15925248 | tf_op jit(solution)/shard_map/all_gather | solution.py:64
  46.3 182.4 %reduce-scatter.2.cloned.1.call-start = ((), (), s32[]{:S(2)}) async-start(), calls=%async_computation.3 | async-start | bytes 15925248 | tf_op jit(solution)/shard_map/reduce_scatter | solution.py:66
  119.5 11.4 %copy-start.5 = (bf16[128,24,2304]{2,0,1:T(8,128)(2,1)S(1)}, bf16[128,24,2304]{2,0,1:T(8,128)(2,1)}, u32[]{:S(2)}) copy-start(bf16[128,24,2304]{2,0,1:T(8,128)(2,1)} %all-gather.3.cloned.1.call-done) | copy-start | bytes 42467332
  119.5 11.4 %copy-start.6 = (bf16[1,2304,480]{1,2,0:T(8,128)(2,1)S(1)}, bf16[1,2304,480]{1,2,0:T(8,128)(2,1)}, u32[]{:S(2)}) copy-start(bf16[1,2304,480]{1,2,0:T(8,128)(2,1)} %param.11) | copy-start | bytes 6635524
  232.0 7.1 %copy-start.2 = (s32[64,2]{0,1:T(2,128)S(1)}, s32[64,2]{0,1:T(2,128)}, u32[]{:S(2)}) copy-start(s32[64,2]{0,1:T(2,128)} %param.8) | copy-start | bytes 1540
  232.0 7.5 %copy-start.3 = (f32[64,2]{0,1:T(2,128)S(1)}, f32[64,2]{0,1:T(2,128)}, u32[]{:S(2)}) copy-start(f32[64,2]{0,1:T(2,128)} %param.9) | copy-start | bytes 1540
  232.0 30.9 %all-to-all-start.1 = ((bf16[16,1,24,2304]{3,2,1,0:T(8,128)(2,1)}), bf16[16,1,24,2304]{3,2,1,0:T(8,128)(2,1)}, u32[]{:S(2)}, u32[]{:S(2)}) async-start(bf16[16,1,24,2304]{3,2,1,0:T(8,128)(2,1)} %copy.37), calls=%async_computation.2 | async-start | bytes 3538944 | tf_op jit(solution)/shard_map/all_to_all | solution.py:74
  238.9 183.0 %all-reduce.2.cloned.1.call-start = ((), (), s32[]{:S(2)}) async-start(), calls=%async_computation.4 | async-start | bytes 589824 | tf_op jit(solution)/shard_map/psum | solution.py:90
  270.0 6.3 %copy-start.4 = (s32[64]{0:T(128)S(1)}, s32[64]{0:T(128)}, u32[]{:S(2)}) copy-start(s32[64]{0:T(128)} %param.10) | copy-start | bytes 772
  276.3 147.3 %copy-start.1 = (bf16[64,2304]{1,0:T(8,128)(2,1)}, bf16[64,2304]{1,0:T(8,128)(2,1)S(1)}, u32[]{:S(2)}) copy-start(bf16[64,2304]{1,0:T(8,128)(2,1)S(1)} %fusion.11) | copy-start | bytes 884740
Sparse Core Ops, SparseCore 0:
  46.5 72.9 all-gather.2
  149.4 79.3 reduce-scatter.1
  277.4 144.4 all-reduce.1
where the time goes:
time: 431 us; the launch traced here: 430 us
  waiting for transfers between devices  252 us (58%)
  blocking collectives  101 us (23%)
  matrix products  32 us (7%)
  between operations  13.9 us (3%)
  local copies, waits for them, and re-layouts  12.5 us (3%)
  other arithmetic  11.7 us (3%)
  starting transfers between devices  7.18 us (2%)
    reduce_scatter x1, waiting for transfers between devices, shards(): lax.psum_scatter(jnp.einsum('nacf,afd->nacd', hidden, w_down, preferred_e...  79.5 us
    psum x1, waiting for transfers between devices, shards(): lax.psum((seq_sums, seq_counts), ('dp', 'tensor', 'expert'))  75.9 us
    all_gather x1, waiting for transfers between devices, shards(): lax.all_gather(local_rows, ('dp', 'tensor'), axis=0, tiled=True)  73.1 us
    psum x1, blocking collectives, shards(): lax.psum((seq_sums, seq_counts), ('dp', 'tensor', 'expert'))  68.6 us
    all_to_all x1, blocking collectives, shards(): lax.all_to_all(send_rows, 'expert', split_axis=0, concat_axis=0, tiled=True)  32.4 us
    all_to_all x1, waiting for transfers between devices, shards(): lax.all_to_all(summed, 'expert', split_axis=0, concat_axis=0, tiled=True)  23.3 us
    dot_general x1, matrix products, expert_hidden(): jnp.einsum('nacd,adf->nacf', row_block, w_up, preferred_element_type=jnp....  11.4 us
    dot_general x1, matrix products, shards(): jnp.einsum('nacf,afd->nacd', hidden, w_down, preferred_element_type=jnp.f...  10.3 us
  transfers between devices with their start and end apart: 4, of which 4 were waited for; matrix products, arithmetic and copies ran while one was open for 0% of the time, Pallas kernels for 0%

commit v1 on v0

--- a/solution.py
+++ b/solution.py
@@ -60,9 +60,14 @@
     send_rows = fan_out(slot_rows, replicas)
     received = lax.all_to_all(send_rows, "expert", split_axis=0, concat_axis=0, tiled=True)
     local_rows = received.reshape(experts_axis, per_device, CAP, width)
-    hidden = expert_hidden(
-        lax.all_gather(local_rows, ("dp", "tensor"), axis=0, tiled=True), w_gate, w_up
-    )
+
+    def rest_quotas(message, axis_tag):
+        nodes = []
+        for _ in range(lax.axis_size(axis_tag)):
+            nodes.append(message)
+        return jnp.concatenate(lax.all_to_all(jnp.stack(nodes), axis_tag, 0, 0), axis=0)
+
+    hidden = expert_hidden(rest_quotas(local_rows, axis_tag=("dp", "tensor")), w_gate, w_up)
     summed = lax.psum_scatter(
         jnp.einsum("nacf,afd->nacd", hidden, w_down, preferred_element_type=jnp.float32).astype(
             jnp.bfloat16

time: 431 us -> 515 us (1.19)
  blocking collectives: 101 us -> 264 us
  waiting for transfers between devices: 252 us -> 175 us
    all_to_all x0 -> x1, blocking collectives: none -> 164 us  [rest_quotas(): lax.all_to_all(jnp.stack(nodes), axis_tag, 0, 0)]
    all_gather x1 -> x0, waiting for transfers between devices: 73.1 us -> none  [shards(): lax.all_gather(local_rows, ('dp', 'tensor'), axis=0, tiled=True)]
  transfers between devices with their start and end apart: 4 -> 3, of which waited for: 4 -> 3; matrix products, arithmetic and copies ran while one was open for 0% -> 0% of each run, Pallas kernels for 0% -> 0%
where the time goes in v1:
time: 515 us; the launch traced here: 514 us
  blocking collectives  264 us (51%)
  waiting for transfers between devices  175 us (34%)
  matrix products  27.7 us (5%)
  local copies, waits for them, and re-layouts  14.5 us (3%)
  between operations  14.2 us (3%)
  other arithmetic  11.7 us (2%)
  starting transfers between devices  7.12 us (1%)
    all_to_all x1, blocking collectives, rest_quotas(): lax.all_to_all(jnp.stack(nodes), axis_tag, 0, 0)  164 us
    psum x1, waiting for transfers between devices, shards(): lax.psum((seq_sums, seq_counts), ('dp', 'tensor', 'expert'))  75.9 us
    reduce_scatter x1, waiting for transfers between devices, shards(): lax.psum_scatter(jnp.einsum('nacf,afd->nacd', hidden, w_down, preferred_e...  75.4 us
    psum x1, blocking collectives, shards(): lax.psum((seq_sums, seq_counts), ('dp', 'tensor', 'expert'))  68.5 us
    all_to_all x1, blocking collectives, shards(): lax.all_to_all(send_rows, 'expert', split_axis=0, concat_axis=0, tiled=True)  32.4 us
    all_to_all x1, waiting for transfers between devices, shards(): lax.all_to_all(summed, 'expert', split_axis=0, concat_axis=0, tiled=True)  23.3 us
  transfers between devices with their start and end apart: 3, of which 3 were waited for; matrix products, arithmetic and copies ran while one was open for 0% of the time, Pallas kernels for 0%

profile of v1, /device:TPU:1, one launch (start us, length us, event | category | flops | bytes accessed | tf_op | source)
XLA Modules:
  0.0 514.4 jit_solution(14627796124889038940)
XLA Ops:
  7.2 0.0 copy-start
  7.2 0.0 reduce-scatter.2.cloned.1.call-start
  7.2 0.9 copy.35
  8.1 0.1 reshape.119
  8.3 0.1 fusion.14
  8.4 0.2 reduce_window_sum.11
  8.5 0.2 select_reduce_fusion
  8.7 0.1 reduce_sum.59
  8.9 0.1 copy.36
  8.9 0.7 compare_and_fusion
  9.6 0.1 convert_reduce_fusion.1
  9.7 1.1 fusion.9
  10.9 1.4 convolution_convert_fusion
  12.3 0.1 broadcast_in_dim.13
  12.4 32.4 %all_to_all.19 = bf16[16,24,2304]{2,1,0:T(8,128)(2,1)S(1)} all-to-all(bf16[16,24,2304]{2,1,0:T(8,128)(2,1)S(1)} %bitcast.66), channel_id=1, replica_groups=mesh['dp'=4,'tensor'=2,'expert'=16] {'expert'}, dimensions={0} | all-to-all | bytes 3538944 | tf_op jit(solution)/shard_map/all_to_all | solution.py:61
  44.8 0.3 copy.38
  45.1 1.2 stack.3
  46.3 163.6 %all_to_all.20 = bf16[8,16,1,24,2304]{4,1,3,2,0:T(8,128)(2,1)S(1)} all-to-all(bf16[8,16,1,24,2304]{4,1,3,2,0:T(8,128)(2,1)S(1)} %stack.3), channel_id=1, replica_groups=mesh['dp'=4,'tensor'=2,'expert'=16] {'dp','tensor'}, dimensions={0} | all-to-all | bytes 28311552 | tf_op jit(solution)/shard_map/all_to_all | solution.py:68
  209.9 1.9 copy.39
  211.8 0.0 copy-done.5
  211.9 0.0 copy-start.6
  211.9 7.0 %fusion.6 = f32[128,24,480]{0,2,1:T(8,128)S(1)} fusion(bf16[128,24,2304]{2,0,1:T(8,128)(2,1)S(1)} %bitcast.64, bf16[1,2304,480]{1,2,0:T(8,128)(2,1)S(1)} %copy-done.5), kind=kOutput, calls=%fused_computation.13 | convolution fusion | flops 6794772480 | bytes 22265856 | tf_op jit(solution)/shard_map/nacd,adf->nacf/dot_general | solution.py:45
  218.9 0.0 copy-done.6
  218.9 8.1 %fusion = bf16[128,1,24,480]{0,3,2,1:T(8,128)(2,1)S(1)} fusion(f32[128,24,480]{0,2,1:T(8,128)S(1)} %fusion.6, bf16[128,24,2304]{2,0,1:T(8,128)(2,1)S(1)} %bitcast.65, bf16[1,2304,480]{1,2,0:T(8,128)(2,1)S(1)} %copy-done.6), kind=kOutput, calls=%fused_computation.3 | convolution fusion | flops 6803619840 | bytes 25214976 | tf_op jit(solution)/shard_map/nacd,adf->nacf/dot_general | solution.py:44
  227.0 10.3 %convert_bitcast_fusion = bf16[128,1,24,2304]{3,0,2,1:T(8,128)(2,1)} fusion(bf16[128,1,24,480]{0,3,2,1:T(8,128)(2,1)S(1)} %fusion, bf16[1,480,2304]{2,1,0:T(8,128)(2,1)S(1)} %copy-done), kind=kOutput, calls=%fused_computation.1 | convolution fusion | flops 6801850368 | bytes 19316736 | tf_op jit(solution)/shard_map/nacf,afd->nacd/dot_general | solution.py:72
  237.3 0.0 reduce-scatter.2.cloned.1.call-update
  237.3 75.4 %reduce-scatter.2.cloned.1.call-done = bf16[16,1,24,2304]{3,0,2,1:T(8,128)(2,1)} async-done(((bf16[128,1,24,2304]{3,0,2,1:T(8,128)(2,1)}), bf16[16,1,24,2304]{3,0,2,1:T(8,128)(2,1)}) %reduce-scatter.2.cloned.1.call-update) | async-done | bytes 1769488 | tf_op jit(solution)/shard_map/reduce_scatter | solution.py:71
  312.7 3.2 copy.40
  315.9 6.9 %all-to-all-start.2 = ((bf16[16,1,24,2304]{3,2,1,0:T(8,128)(2,1)}), bf16[16,1,24,2304]{3,2,1,0:T(8,128)(2,1)}, u32[]{:S(2)}, u32[]{:S(2)}) async-start(bf16[16,1,24,2304]{3,2,1,0:T(8,128)(2,1)} %copy.40), calls=%async_computation.3 | async-start | bytes 3538944 | tf_op jit(solution)/shard_map/all_to_all | solution.py:79
  322.8 0.2 all-reduce.2.cloned.1.call-start
  323.0 0.1 copy.43
  323.1 0.1 mul.61
  323.3 0.1 copy.37
  323.4 0.1 copy.34
  323.5 23.3 %all-to-all-done.2 = bf16[16,1,24,2304]{3,2,1,0:T(8,128)(2,1)} async-done(((bf16[16,1,24,2304]{3,2,1,0:T(8,128)(2,1)}), bf16[16,1,24,2304]{3,2,1,0:T(8,128)(2,1)}, u32[]{:S(2)}, u32[]{:S(2)}) %all-to-all-start.2) | async-done | bytes 1769504 | tf_op jit(solution)/shard_map/all_to_all | solution.py:79
  346.9 3.2 convert_reduce_fusion
  350.0 4.0 gather_fusion
  354.0 2.0 gather.7
  356.0 3.2 multiply_reduce_fusion
  359.3 1.0 fusion.11
  360.3 0.0 copy-start.1
  360.3 0.9 fusion.17
  361.2 0.0 all-reduce.2.cloned.1.call-update
  361.2 0.1 convert_reduce_fusion.2
  361.3 68.5 %psum.15 = f32[32]{0:T(128)S(1)} all-reduce(f32[32]{0:T(128)S(1)} %convert_reduce_fusion.2), channel_id=1, replica_groups=mesh['dp'=4,'tensor'=2,'expert'=16] {'dp','tensor','expert'}, use_global_device_ids=true, to_apply=%region_9.10 | all-reduce | flops 32 | bytes 256 | tf_op jit(solution)/shard_map/psum | solution.py:95
  429.8 75.9 %all-reduce.2.cloned.1.call-done = f32[32,2304]{1,0:T(8,128)} async-done(((f32[32,2304]{1,0:T(8,128)}), f32[32,2304]{1,0:T(8,128)}) %all-reduce.2.cloned.1.call-update) | async-done | bytes 294928 | tf_op jit(solution)/shard_map/psum | solution.py:95
  505.7 1.8 broadcast_divide_fusion
  507.5 0.0 copy-done.1
  (12 shorter events, 0.0 us)
Async XLA Ops:
  7.2 219.8 %copy-start = (bf16[1,480,2304]{2,1,0:T(8,128)(2,1)S(1)}, bf16[1,480,2304]{2,1,0:T(8,128)(2,1)}, u32[]{:S(2)}) copy-start(bf16[1,480,2304]{2,1,0:T(8,128)(2,1)} %param.13) | copy-start | bytes 6635524
  7.2 305.5 %reduce-scatter.2.cloned.1.call-start = ((), (), s32[]{:S(2)}) async-start(), calls=%async_computation.4 | async-start | bytes 15925248 | tf_op jit(solution)/shard_map/reduce_scatter | solution.py:71
  209.9 1.9 copy-start.5
  211.9 7.1 %copy-start.6 = (bf16[1,2304,480]{1,2,0:T(8,128)(2,1)S(1)}, bf16[1,2304,480]{1,2,0:T(8,128)(2,1)}, u32[]{:S(2)}) copy-start(bf16[1,2304,480]{1,2,0:T(8,128)(2,1)} %param.11) | copy-start | bytes 6635524
  315.9 7.1 %copy-start.2 = (s32[64,2]{0,1:T(2,128)S(1)}, s32[64,2]{0,1:T(2,128)}, u32[]{:S(2)}) copy-start(s32[64,2]{0,1:T(2,128)} %param.8) | copy-start | bytes 1540
  315.9 7.5 %copy-start.3 = (f32[64,2]{0,1:T(2,128)S(1)}, f32[64,2]{0,1:T(2,128)}, u32[]{:S(2)}) copy-start(f32[64,2]{0,1:T(2,128)} %param.9) | copy-start | bytes 1540
  315.9 30.9 %all-to-all-start.2 = ((bf16[16,1,24,2304]{3,2,1,0:T(8,128)(2,1)}), bf16[16,1,24,2304]{3,2,1,0:T(8,128)(2,1)}, u32[]{:S(2)}, u32[]{:S(2)}) async-start(bf16[16,1,24,2304]{3,2,1,0:T(8,128)(2,1)} %copy.40), calls=%async_computation.3 | async-start | bytes 3538944 | tf_op jit(solution)/shard_map/all_to_all | solution.py:79
  322.8 183.0 %all-reduce.2.cloned.1.call-start = ((), (), s32[]{:S(2)}) async-start(), calls=%async_computation.5 | async-start | bytes 589824 | tf_op jit(solution)/shard_map/psum | solution.py:95
  354.0 6.3 %copy-start.4 = (s32[64]{0:T(128)S(1)}, s32[64]{0:T(128)}, u32[]{:S(2)}) copy-start(s32[64]{0:T(128)} %param.10) | copy-start | bytes 772
  360.3 147.2 %copy-start.1 = (bf16[64,2304]{1,0:T(8,128)(2,1)}, bf16[64,2304]{1,0:T(8,128)(2,1)S(1)}, u32[]{:S(2)}) copy-start(bf16[64,2304]{1,0:T(8,128)(2,1)S(1)} %fusion.11) | copy-start | bytes 884740
Sparse Core Ops, SparseCore 0:
  237.4 75.2 reduce-scatter.1
  361.4 144.3 all-reduce.1
